TPU v7x, 512 devices: a whole 4x4x16 slice. The times are simulated.
512 devices in a mesh: outer: 16 (over x, y_lo, core), inner: 32 (over y_hi, z).
Axes of the slice: x: 4, y: 4 (y_hi: 2, y_lo: 2; y = y_hi * 2 + y_lo), z: 16, core: 2. Of those that a mesh axis runs over, the one named last changes fastest.
Arguments:
- queries: bfloat16 [262144, 1024], P(('outer', 'inner')), may hold values from -1000 to 1000
- kv_codes: bfloat16 [262144, 256], P(('outer', 'inner')), may hold values from -4 to 4
- scale_exp: int32 [2048, 2], P(('outer', 'inner')), may hold values from -1 to 1
- positions: int32 [262144], P(('outer', 'inner')), may hold values from 0 to 262143, as said below
Outputs:
- attended: bfloat16 [262144, 1024], P(('outer', 'inner'))
Inputs may be any that keep to these rules, and one draw needn't show every extreme that they name: Every position occurs once; each block of 512 rows is two runs of 256 rows holding consecutive rising positions, each run starting at a multiple of 256.
All inputs are finite; a program needn't handle non-finite values.
Results may differ from a plain program's by a relative error of at most 0.0065.
Values may be sent and summed in bfloat16 or wider, within the bound.
A program may use at most 64 MiB of HBM per device.

v0:
```python
import jax
import jax.numpy as jnp
from jax import lax
from jax.sharding import PartitionSpec as P

HEADS = 8
HEAD_DIM = 128
SCALE_ROWS = 128


def from_behind(block, axis, distance):
    devices = range(lax.axis_size(axis))
    route = [((i - distance) % len(devices), i) for i in devices]
    return lax.ppermute(block, axis, route)


def dequantize(codes, exponents):
    factors = jnp.repeat(jnp.exp2(exponents.astype(jnp.float32)), SCALE_ROWS, axis=0)
    keys = (codes[:, :HEAD_DIM].astype(jnp.float32) * factors[:, 0:1]).astype(jnp.bfloat16)
    values = (codes[:, HEAD_DIM:].astype(jnp.float32) * factors[:, 1:2]).astype(jnp.bfloat16)
    return (keys, values)


def partial_sums(query_rows, query_pos, codes, exponents, key_pos):
    keys, values = dequantize(codes, exponents)
    heads_view = query_rows.reshape(query_rows.shape[0], HEADS, HEAD_DIM)
    scores = jnp.einsum(
        "thd,kd->thk", heads_view, keys, preferred_element_type=jnp.float32
    ) * HEAD_DIM ** (-0.5)
    visible = key_pos[None, None, :] <= query_pos[:, None, None]
    scores = jnp.where(visible, scores, -1e30)
    top = jnp.max(scores, axis=2)
    weights = jnp.where(visible, jnp.exp(scores - top[:, :, None]), 0.0)
    total = jnp.sum(weights, axis=2)
    numer = jnp.einsum(
        "thk,kd->thd", weights.astype(jnp.bfloat16), values, preferred_element_type=jnp.float32
    )
    return (numer, top, total)


def combine(first, second):
    top = jnp.maximum(first[1], second[1])
    scale_one = jnp.exp(first[1] - top)
    scale_two = jnp.exp(second[1] - top)
    numer = first[0] * scale_one[:, :, None] + second[0] * scale_two[:, :, None]
    total = first[2] * scale_one + second[2] * scale_two
    return (numer, top, total)


def local(queries, kv_codes, scale_exp, positions):
    state = partial_sums(queries, positions, kv_codes, scale_exp, positions)
    moving = (kv_codes, scale_exp, positions)
    for step in range(1, 4):
        moving = from_behind((moving[0], moving[1], moving[2]), "inner", 1)
        state = combine(state, partial_sums(queries, positions, moving[0], moving[1], moving[2]))
    handed = from_behind((kv_codes, scale_exp, positions), "outer", 1)
    state = combine(state, partial_sums(queries, positions, handed[0], handed[1], handed[2]))
    attended = state[0] / state[2][:, :, None]
    return attended.astype(jnp.bfloat16).reshape(queries.shape[0], HEADS * HEAD_DIM)


def solution(mesh):
    in_specs = (
        P(("outer", "inner"), None),
        P(("outer", "inner"), None),
        P(("outer", "inner"), None),
        P(("outer", "inner")),
    )
    out_specs = P(("outer", "inner"), None)
    return jax.shard_map(local, mesh=mesh, in_specs=in_specs, out_specs=out_specs, check_vma=False)
```

profile of v0, /device:TPU:6, one launch (start us, length us, event | category | flops | bytes accessed | tf_op | source)
XLA Modules:
  0.0 105.0 jit_solution(12794237781507126883)
XLA Ops:
  0.0 2.0 %collective-permute-start.11 = (s32[4,2]{0,1:T(2,128)}, s32[4,2]{0,1:T(2,128)S(1)}, u32[]{:S(2)}, u32[]{:S(2)}) collective-permute-start(s32[4,2]{0,1:T(2,128)} %param.6), channel_id=1, source_target_pairs={{480,0},{0,32},{32,64},{64,96},{96,128},{128,160},{160,192},{192,2... | collective-permute-start | bytes 104 | tf_op jit(solution)/shard_map/ppermute | solution.py:14
  2.1 3.8 %collective-permute-start.2 = (s32[4,2]{0,1:T(2,128)}, s32[4,2]{0,1:T(2,128)S(1)}, u32[]{:S(2)}, u32[]{:S(2)}) collective-permute-start(s32[4,2]{0,1:T(2,128)} %param.6), channel_id=1, source_target_pairs={{31,0},{0,1},{1,2},{2,3},{3,4},{4,5},{5,6},{6,7},{7,8},{8,9},{9,10... | collective-permute-start | bytes 104 | tf_op jit(solution)/shard_map/ppermute | solution.py:14
  5.9 3.3 %collective-permute-start.9 = (s32[512]{0:T(512)}, s32[512]{0:T(512)S(1)}, u32[]{:S(2)}, u32[]{:S(2)}) collective-permute-start(s32[512]{0:T(512)} %param.7), channel_id=1, source_target_pairs={{480,0},{0,32},{32,64},{64,96},{96,128},{128,160},{160,192},{192,2... | collective-permute-start | bytes 6152 | tf_op jit(solution)/shard_map/ppermute | solution.py:14
  9.2 3.8 %collective-permute-start = (s32[512]{0:T(512)}, s32[512]{0:T(512)S(1)}, u32[]{:S(2)}, u32[]{:S(2)}) collective-permute-start(s32[512]{0:T(512)} %param.7), channel_id=1, source_target_pairs={{31,0},{0,1},{1,2},{2,3},{3,4},{4,5},{5,6},{6,7},{7,8},{8,9},{9,10... | collective-permute-start | bytes 6152 | tf_op jit(solution)/shard_map/ppermute | solution.py:14
  15.8 3.8 %collective-permute-start.1 = (bf16[512,256]{1,0:T(8,128)(2,1)}, bf16[512,256]{1,0:T(8,128)(2,1)S(1)}, u32[]{:S(2)}, u32[]{:S(2)}) collective-permute-start(bf16[512,256]{1,0:T(8,128)(2,1)} %param.5), channel_id=1, source_target_pairs={{31,0},{0,1},{1,2},{2,3},{3,4},{4,5},{5,6},{6,7},{7,8},{8,9},{9,10... | collective-permute-start | bytes 786440 | tf_op jit(solution)/shard_map/ppermute | solution.py:14
  19.8 5.0 %collective-permute-start.5 = (s32[4,2]{0,1:T(2,128)S(1)}, s32[4,2]{0,1:T(2,128)S(1)}, u32[]{:S(2)}, u32[]{:S(2)}) collective-permute-start(s32[4,2]{0,1:T(2,128)S(1)} %collective-permute-done.2), channel_id=1, source_target_pairs={{31,0},{0,1},{1,2},{2,3},{3,4},{4,5},{5,6},{6,7},{7,8},{8,9},{9,10... | collective-permute-start | bytes 104 | tf_op jit(solution)/shard_map/ppermute | solution.py:14
  24.8 8.5 %collective-permute-done.5 = s32[4,2]{0,1:T(2,128)S(1)} collective-permute-done((s32[4,2]{0,1:T(2,128)S(1)}, s32[4,2]{0,1:T(2,128)S(1)}, u32[]{:S(2)}, u32[]{:S(2)}) %collective-permute-start.5) | collective-permute-done | bytes 64 | tf_op jit(solution)/shard_map/ppermute | solution.py:14
  35.3 7.1 %collective-permute-done.8 = s32[4,2]{0,1:T(2,128)S(1)} collective-permute-done((s32[4,2]{0,1:T(2,128)S(1)}, s32[4,2]{0,1:T(2,128)S(1)}, u32[]{:S(2)}, u32[]{:S(2)}) %collective-permute-start.8) | collective-permute-done | bytes 64 | tf_op jit(solution)/shard_map/ppermute | solution.py:14
  44.5 7.1 %collective-permute-done.3 = s32[512]{0:T(512)S(1)} collective-permute-done((s32[512]{0:T(512)S(1)}, s32[512]{0:T(512)S(1)}, u32[]{:S(2)}, u32[]{:S(2)}) %collective-permute-start.3) | collective-permute-done | bytes 2080 | tf_op jit(solution)/shard_map/ppermute | solution.py:14
  53.5 7.1 %collective-permute-done.6 = s32[512]{0:T(512)S(1)} collective-permute-done((s32[512]{0:T(512)S(1)}, s32[512]{0:T(512)S(1)}, u32[]{:S(2)}, u32[]{:S(2)}) %collective-permute-start.6) | collective-permute-done | bytes 2080 | tf_op jit(solution)/shard_map/ppermute | solution.py:14
  62.3 2.6 %fusion = (f32[512,8]{0,1:T(8,128)S(1)}, f32[512,512,8]{1,0,2:T(8,128)S(1)}) fusion(pred[512,512]{0,1:T(8,128)(4,1)S(1)} %get-tuple-element.27, f32[512]{0:T(512)S(1)} %bitcast.188, bf16[512,256]{1,0:T(8,128)(2,1)} %param.5, bf16[512,1024]{1,0:T(8,128)(2,1)S(1)} %copy-done), kind=kOutput, calls=%fused_computation.10 | convolution fusion | flops 543354880 | bytes 9848832 | tf_op jit(solution)/shard_map/thd,kd->thk/dot_general | solution.py:27
  64.9 2.2 %fusion.23 = f32[512,8,128]{0,2,1:T(8,128)S(1)} fusion(f32[512,512,8]{1,0,2:T(8,128)S(1)} %get-tuple-element.36, f32[512,8]{0,1:T(8,128)S(1)} %get-tuple-element.35, pred[512,512]{0,1:T(8,128)(4,1)S(1)} %get-tuple-element.27, f32[512]{0:T(512)S(1)} %bitcast.195, bf16[512,256]{1,0:T(8,128)(2,1)S(1)} %copy-done.1), kind=kOutput, calls=%fused_computation.29 | convolution fusion | flops 547553280 | bytes 10897408 | tf_op jit(solution)/shard_map/thk,kd->thd/dot_general | solution.py:35
  67.1 2.0 %fusion.5 = f32[512,8]{0,1:T(8,128)S(1)} fusion(f32[512,512,8]{1,0,2:T(8,128)S(1)} %get-tuple-element.36, f32[512,8]{0,1:T(8,128)S(1)} %get-tuple-element.35, pred[512,512]{0,1:T(8,128)(4,1)S(1)} %get-tuple-element.27), kind=kLoop, calls=%fused_computation.15 | loop fusion | flops 10481664 | bytes 8683520 | tf_op jit(solution)/shard_map/reduce_sum | solution.py:34
  70.8 2.0 %fusion.13 = f32[512,8]{0,1:T(8,128)S(1)} fusion(f32[512,512,8]{1,0,2:T(8,128)S(1)} %get-tuple-element.30, f32[512,8]{0,1:T(8,128)S(1)} %get-tuple-element.29, pred[512,512]{0,1:T(8,128)(4,1)S(1)} %get-tuple-element.26), kind=kLoop, calls=%fused_computation.23 | loop fusion | flops 10481664 | bytes 8683520 | tf_op jit(solution)/shard_map/reduce_sum | solution.py:34
  72.9 2.1 %collective-permute-start.4 = (bf16[512,256]{1,0:T(8,128)(2,1)S(1)}, bf16[512,256]{1,0:T(8,128)(2,1)S(1)}, u32[]{:S(2)}, u32[]{:S(2)}) collective-permute-start(bf16[512,256]{1,0:T(8,128)(2,1)S(1)} %collective-permute-done.1), channel_id=1, source_target_pairs={{31,0},{0,1},{1,2},{2,3},{3,4},{4,5},{5,6},{6,7},{7,8},{8,9},{9,10... | collective-permute-start | bytes 786440 | tf_op jit(solution)/shard_map/ppermute | solution.py:14
  75.0 2.2 %fusion.15 = f32[512,8,128]{0,2,1:T(8,128)S(1)} fusion(f32[512,512,8]{1,0,2:T(8,128)S(1)} %get-tuple-element.30, f32[512,8]{0,1:T(8,128)S(1)} %get-tuple-element.29, pred[512,512]{0,1:T(8,128)(4,1)S(1)} %get-tuple-element.26, bf16[512,256]{1,0:T(8,128)(2,1)S(1)} %collective-permute-done.10, f32[512]{0:T(512)S(1)} %bitcast.192), kind=kOutput, calls=%fused_computation.25 | convolution fusion | flops 547553280 | bytes 10897408 | tf_op jit(solution)/shard_map/thk,kd->thd/dot_general | solution.py:35
  78.8 2.2 %fusion.21 = f32[512,8,128]{0,2,1:T(8,128)S(1)} fusion(f32[512,512,8]{1,0,2:T(8,128)S(1)} %get-tuple-element.34, f32[512,8]{0,1:T(8,128)S(1)} %get-tuple-element.33, pred[512,512]{0,1:T(8,128)(4,1)S(1)} %get-tuple-element.28, bf16[512,256]{1,0:T(8,128)(2,1)S(1)} %collective-permute-done.1, f32[512]{0:T(512)S(1)} %bitcast.194), kind=kOutput, calls=%fused_computation.28 | convolution fusion | flops 547553280 | bytes 10897408 | tf_op jit(solution)/shard_map/thk,kd->thd/dot_general | solution.py:35
  81.0 2.0 %fusion.7 = f32[512,8]{0,1:T(8,128)S(1)} fusion(f32[512,512,8]{1,0,2:T(8,128)S(1)} %get-tuple-element.34, f32[512,8]{0,1:T(8,128)S(1)} %get-tuple-element.33, pred[512,512]{0,1:T(8,128)(4,1)S(1)} %get-tuple-element.28), kind=kLoop, calls=%fused_computation.17 | loop fusion | flops 10481664 | bytes 8683520 | tf_op jit(solution)/shard_map/reduce_sum | solution.py:34
  84.7 2.1 %collective-permute-start.7 = (bf16[512,256]{1,0:T(8,128)(2,1)S(1)}, bf16[512,256]{1,0:T(8,128)(2,1)S(1)}, u32[]{:S(2)}, u32[]{:S(2)}) collective-permute-start(bf16[512,256]{1,0:T(8,128)(2,1)S(1)} %collective-permute-done.4), channel_id=1, source_target_pairs={{31,0},{0,1},{1,2},{2,3},{3,4},{4,5},{5,6},{6,7},{7,8},{8,9},{9,10... | collective-permute-start | bytes 786440 | tf_op jit(solution)/shard_map/ppermute | solution.py:14
  88.5 2.2 %fusion.19 = f32[512,8,128]{0,2,1:T(8,128)S(1)} fusion(f32[512,512,8]{1,0,2:T(8,128)S(1)} %get-tuple-element.32, f32[512,8]{0,1:T(8,128)S(1)} %get-tuple-element.31, pred[512,512]{0,1:T(8,128)(4,1)S(1)} %get-tuple-element.25, bf16[512,256]{1,0:T(8,128)(2,1)S(1)} %collective-permute-done.4, f32[512]{0:T(512)S(1)} %bitcast.193), kind=kOutput, calls=%fused_computation.27 | convolution fusion | flops 547553280 | bytes 10897408 | tf_op jit(solution)/shard_map/thk,kd->thd/dot_general | solution.py:35
  90.7 2.0 %fusion.9 = f32[512,8]{0,1:T(8,128)S(1)} fusion(f32[512,512,8]{1,0,2:T(8,128)S(1)} %get-tuple-element.32, f32[512,8]{0,1:T(8,128)S(1)} %get-tuple-element.31, pred[512,512]{0,1:T(8,128)(4,1)S(1)} %get-tuple-element.25), kind=kLoop, calls=%fused_computation.19 | loop fusion | flops 10481664 | bytes 8683520 | tf_op jit(solution)/shard_map/reduce_sum | solution.py:34
  92.7 3.9 %collective-permute-done.7 = bf16[512,256]{1,0:T(8,128)(2,1)S(1)} collective-permute-done((bf16[512,256]{1,0:T(8,128)(2,1)S(1)}, bf16[512,256]{1,0:T(8,128)(2,1)S(1)}, u32[]{:S(2)}, u32[]{:S(2)}) %collective-permute-start.7) | collective-permute-done | bytes 262176 | tf_op jit(solution)/shard_map/ppermute | solution.py:14
  98.3 2.0 %fusion.11 = f32[512,8]{0,1:T(8,128)S(1)} fusion(f32[512,512,8]{1,0,2:T(8,128)S(1)} %get-tuple-element.38, f32[512,8]{0,1:T(8,128)S(1)} %get-tuple-element.37, pred[512,512]{0,1:T(8,128)(4,1)S(1)} %get-tuple-element.24), kind=kLoop, calls=%fused_computation.21 | loop fusion | flops 10481664 | bytes 8683520 | tf_op jit(solution)/shard_map/reduce_sum | solution.py:34
  100.3 3.4 %divide_convert_fusion = bf16[512,8,128]{0,2,1:T(8,128)(2,1)S(1)} fusion(f32[512,8,128]{0,2,1:T(8,128)S(1)} %fusion.15, f32[512,8,128]{0,2,1:T(8,128)S(1)} %fusion.19, f32[512,8,128]{0,2,1:T(8,128)S(1)} %fusion.21, f32[512,8,128]{0,2,1:T(8,128)S(1)} %fusion.23, f32[512,512,8]{1,0,2:T(8,128)S(1)} %get-tuple-element.38, f32[512,8]{0,1:T(8,128)S(1)} %get-tuple-element.37, ...), kind=kOutput, calls=%fused_computation.35 | convolution fusion | flops 554893312 | bytes 18384896 | tf_op jit(solution)/shard_map/thk,kd->thd/dot_general | solution.py:35
  (42 shorter events, 20.1 us)
Async XLA Ops:
  0.0 62.3 %copy-start = (bf16[512,1024]{1,0:T(8,128)(2,1)S(1)}, bf16[512,1024]{1,0:T(8,128)(2,1)}, u32[]{:S(2)}) copy-start(bf16[512,1024]{1,0:T(8,128)(2,1)} %param.4) | copy-start | bytes 3145732
  0.0 64.9 %copy-start.1 = (bf16[512,256]{1,0:T(8,128)(2,1)S(1)}, bf16[512,256]{1,0:T(8,128)(2,1)}, u32[]{:S(2)}) copy-start(bf16[512,256]{1,0:T(8,128)(2,1)} %param.5) | copy-start | bytes 786436
  0.0 15.7 %collective-permute-start.11 = (s32[4,2]{0,1:T(2,128)}, s32[4,2]{0,1:T(2,128)S(1)}, u32[]{:S(2)}, u32[]{:S(2)}) collective-permute-start(s32[4,2]{0,1:T(2,128)} %param.6), channel_id=1, source_target_pairs={{480,0},{0,32},{32,64},{64,96},{96,128},{128,160},{160,192},{192,2... | collective-permute-start | bytes 104 | tf_op jit(solution)/shard_map/ppermute | solution.py:14
  2.1 17.6 %collective-permute-start.2 = (s32[4,2]{0,1:T(2,128)}, s32[4,2]{0,1:T(2,128)S(1)}, u32[]{:S(2)}, u32[]{:S(2)}) collective-permute-start(s32[4,2]{0,1:T(2,128)} %param.6), channel_id=1, source_target_pairs={{31,0},{0,1},{1,2},{2,3},{3,4},{4,5},{5,6},{6,7},{7,8},{8,9},{9,10... | collective-permute-start | bytes 104 | tf_op jit(solution)/shard_map/ppermute | solution.py:14
  5.9 47.6 %collective-permute-start.9 = (s32[512]{0:T(512)}, s32[512]{0:T(512)S(1)}, u32[]{:S(2)}, u32[]{:S(2)}) collective-permute-start(s32[512]{0:T(512)} %param.7), channel_id=1, source_target_pairs={{480,0},{0,32},{32,64},{64,96},{96,128},{128,160},{160,192},{192,2... | collective-permute-start | bytes 6152 | tf_op jit(solution)/shard_map/ppermute | solution.py:14
  9.2 33.3 %collective-permute-start = (s32[512]{0:T(512)}, s32[512]{0:T(512)S(1)}, u32[]{:S(2)}, u32[]{:S(2)}) collective-permute-start(s32[512]{0:T(512)} %param.7), channel_id=1, source_target_pairs={{31,0},{0,1},{1,2},{2,3},{3,4},{4,5},{5,6},{6,7},{7,8},{8,9},{9,10... | collective-permute-start | bytes 6152 | tf_op jit(solution)/shard_map/ppermute | solution.py:14
  13.0 56.1 %collective-permute-start.10 = (bf16[512,256]{1,0:T(8,128)(2,1)}, bf16[512,256]{1,0:T(8,128)(2,1)S(1)}, u32[]{:S(2)}, u32[]{:S(2)}) collective-permute-start(bf16[512,256]{1,0:T(8,128)(2,1)} %param.5), channel_id=1, source_target_pairs={{480,0},{0,32},{32,64},{64,96},{96,128},{128,160},{160,192},{192,2... | collective-permute-start | bytes 786440 | tf_op jit(solution)/shard_map/ppermute | solution.py:14
  15.8 57.1 %collective-permute-start.1 = (bf16[512,256]{1,0:T(8,128)(2,1)}, bf16[512,256]{1,0:T(8,128)(2,1)S(1)}, u32[]{:S(2)}, u32[]{:S(2)}) collective-permute-start(bf16[512,256]{1,0:T(8,128)(2,1)} %param.5), channel_id=1, source_target_pairs={{31,0},{0,1},{1,2},{2,3},{3,4},{4,5},{5,6},{6,7},{7,8},{8,9},{9,10... | collective-permute-start | bytes 786440 | tf_op jit(solution)/shard_map/ppermute | solution.py:14
  19.8 13.5 %collective-permute-start.5 = (s32[4,2]{0,1:T(2,128)S(1)}, s32[4,2]{0,1:T(2,128)S(1)}, u32[]{:S(2)}, u32[]{:S(2)}) collective-permute-start(s32[4,2]{0,1:T(2,128)S(1)} %collective-permute-done.2), channel_id=1, source_target_pairs={{31,0},{0,1},{1,2},{2,3},{3,4},{4,5},{5,6},{6,7},{7,8},{8,9},{9,10... | collective-permute-start | bytes 104 | tf_op jit(solution)/shard_map/ppermute | solution.py:14
  33.4 9.1 %collective-permute-start.8 = (s32[4,2]{0,1:T(2,128)S(1)}, s32[4,2]{0,1:T(2,128)S(1)}, u32[]{:S(2)}, u32[]{:S(2)}) collective-permute-start(s32[4,2]{0,1:T(2,128)S(1)} %collective-permute-done.5), channel_id=1, source_target_pairs={{31,0},{0,1},{1,2},{2,3},{3,4},{4,5},{5,6},{6,7},{7,8},{8,9},{9,10... | collective-permute-start | bytes 104 | tf_op jit(solution)/shard_map/ppermute | solution.py:14
  42.5 9.1 %collective-permute-start.3 = (s32[512]{0:T(512)S(1)}, s32[512]{0:T(512)S(1)}, u32[]{:S(2)}, u32[]{:S(2)}) collective-permute-start(s32[512]{0:T(512)S(1)} %collective-permute-done), channel_id=1, source_target_pairs={{31,0},{0,1},{1,2},{2,3},{3,4},{4,5},{5,6},{6,7},{7,8},{8,9},{9,10... | collective-permute-start | bytes 6152 | tf_op jit(solution)/shard_map/ppermute | solution.py:14
  51.6 9.1 %collective-permute-start.6 = (s32[512]{0:T(512)S(1)}, s32[512]{0:T(512)S(1)}, u32[]{:S(2)}, u32[]{:S(2)}) collective-permute-start(s32[512]{0:T(512)S(1)} %collective-permute-done.3), channel_id=1, source_target_pairs={{31,0},{0,1},{1,2},{2,3},{3,4},{4,5},{5,6},{6,7},{7,8},{8,9},{9,10... | collective-permute-start | bytes 6152 | tf_op jit(solution)/shard_map/ppermute | solution.py:14
  72.9 11.9 %collective-permute-start.4 = (bf16[512,256]{1,0:T(8,128)(2,1)S(1)}, bf16[512,256]{1,0:T(8,128)(2,1)S(1)}, u32[]{:S(2)}, u32[]{:S(2)}) collective-permute-start(bf16[512,256]{1,0:T(8,128)(2,1)S(1)} %collective-permute-done.1), channel_id=1, source_target_pairs={{31,0},{0,1},{1,2},{2,3},{3,4},{4,5},{5,6},{6,7},{7,8},{8,9},{9,10... | collective-permute-start | bytes 786440 | tf_op jit(solution)/shard_map/ppermute | solution.py:14
  84.7 11.9 %collective-permute-start.7 = (bf16[512,256]{1,0:T(8,128)(2,1)S(1)}, bf16[512,256]{1,0:T(8,128)(2,1)S(1)}, u32[]{:S(2)}, u32[]{:S(2)}) collective-permute-start(bf16[512,256]{1,0:T(8,128)(2,1)S(1)} %collective-permute-done.4), channel_id=1, source_target_pairs={{31,0},{0,1},{1,2},{2,3},{3,4},{4,5},{5,6},{6,7},{7,8},{8,9},{9,10... | collective-permute-start | bytes 786440 | tf_op jit(solution)/shard_map/ppermute | solution.py:14
where the time goes:
time: 106 us; the launch traced here: 105 us
  waiting for transfers between devices  35.4 us (33%)
  starting transfers between devices  33.8 us (32%)
  matrix products  21.2 us (20%)
  other arithmetic  12.6 us (12%)
  local copies, waits for them, and re-layouts  1.75 us (2%)
    ppermute x12, waiting for transfers between devices, from_behind(): return lax.ppermute(block, axis, route)  35.4 us
    ppermute x12, starting transfers between devices, from_behind(): return lax.ppermute(block, axis, route)  33.8 us
    dot_general x5, matrix products, partial_sums(): jnp.einsum('thk,kd->thd', weights.astype(jnp.bfloat16), values, preferred...  12.1 us
    reduce_sum x5, other arithmetic, partial_sums(): total = jnp.sum(weights, axis=2)  10.2 us
    dot_general x5, matrix products, partial_sums(): jnp.einsum('thd,kd->thk', heads_view, keys, preferred_element_type=jnp.fl...  9.14 us
  transfers between devices with their start and end apart: 12, of which 6 were waited for; matrix products, arithmetic and copies ran while one was open for 26% of the time, Pallas kernels for 0%

commit v1 on v0

v1 whole, which is shorter than its diff:
```python
import functools
import math

import jax
import jax.numpy as jnp
from jax import lax
from jax.experimental import pallas as pl
from jax.experimental.pallas import tpu as pltpu
from jax.sharding import PartitionSpec as P

MESH = pl.DeviceIdType.MESH
HEADS = 8
DIM = 128
SPAN = 256
GROUP = 128
BIG = 1e30
SCALE = math.log2(math.e) / math.sqrt(128.0)
BF16 = jnp.bfloat16
F32 = jnp.float32

FORWARD = {2: 6, 4: 7, 6: 8, 7: 9}
CHUNKS = 10


def kernel(
    n_outer, n_inner,
    q_hbm, kv_hbm, exp_ref, pos_ref, out_hbm,
    q_in, kvb, meta, q2, kt, va, acc, mx, bias, stage,
    local_sem, send_sem, recv_sem, msend_sem, mrecv_sem, out_sem,
):
    o, i = lax.axis_index("outer"), lax.axis_index("inner")
    ahead = (o, lax.rem(i + 1, n_inner))
    behind = (o, lax.rem(i + n_inner - 1, n_inner))
    above = (lax.rem(o + 1, n_outer), i)
    below = (lax.rem(o + n_outer - 1, n_outer), i)

    barrier = pltpu.get_barrier_semaphore()
    for peer in (ahead, behind, above, below):
        pl.semaphore_signal(barrier, inc=1, device_id=peer, device_id_type=MESH)

    q_copy = pltpu.make_async_copy(q_hbm, q_in, local_sem.at[0])
    q_copy.start()
    own = []
    for s in range(2):
        own.append(pltpu.make_async_copy(kv_hbm.at[pl.ds(s * SPAN, SPAN)], kvb.at[s], local_sem.at[1 + s]))
        own[s].start()

    for s in range(2):
        for g in range(2):
            for side in range(2):
                e = jnp.full((1, 128), exp_ref[side, 2 * s + g], jnp.int32)
                f = jnp.where(e > 0, 2.0, jnp.where(e < 0, 0.5, 1.0)).astype(F32)
                meta[s, pl.ds(2 * side + g, 1), :] = f
        meta[s, pl.ds(4, 1), :] = jnp.full((1, 128), pos_ref[s * SPAN], jnp.int32).astype(F32)
        meta[s, pl.ds(5, 3), :] = jnp.zeros((3, 128), F32)

    pl.semaphore_wait(barrier, 4)

    def send(src, meta_src, chunk, device):
        pltpu.make_async_remote_copy(
            src_ref=meta_src, dst_ref=meta.at[chunk], send_sem=msend_sem.at[chunk],
            recv_sem=mrecv_sem.at[chunk], device_id=device, device_id_type=MESH,
        ).start()
        pltpu.make_async_remote_copy(
            src_ref=src, dst_ref=kvb.at[chunk], send_sem=send_sem.at[chunk],
            recv_sem=recv_sem.at[chunk], device_id=device, device_id_type=MESH,
        ).start()

    def arrived(chunk):
        pltpu.make_async_remote_copy(
            src_ref=meta.at[chunk], dst_ref=meta.at[chunk], send_sem=msend_sem.at[chunk],
            recv_sem=mrecv_sem.at[chunk], device_id=ahead, device_id_type=MESH,
        ).wait_recv()
        pltpu.make_async_remote_copy(
            src_ref=kvb.at[chunk], dst_ref=kvb.at[chunk], send_sem=send_sem.at[chunk],
            recv_sem=recv_sem.at[chunk], device_id=ahead, device_id_type=MESH,
        ).wait_recv()

    def sent(chunk):
        pltpu.make_async_remote_copy(
            src_ref=meta.at[chunk], dst_ref=meta.at[chunk], send_sem=msend_sem.at[chunk],
            recv_sem=mrecv_sem.at[chunk], device_id=ahead, device_id_type=MESH,
        ).wait_send()
        pltpu.make_async_remote_copy(
            src_ref=kvb.at[chunk], dst_ref=kvb.at[chunk], send_sem=send_sem.at[chunk],
            recv_sem=recv_sem.at[chunk], device_id=ahead, device_id_type=MESH,
        ).wait_send()

    for s in range(2):
        rows = kv_hbm.at[pl.ds(s * SPAN, SPAN)]
        send(rows, meta.at[s], 2 + 2 * s, ahead)
        send(rows, meta.at[s], 3 + 2 * s, above)

    q_copy.wait()
    for h in range(HEADS):
        x = q_in[:, h * DIM : (h + 1) * DIM].astype(F32) * SCALE
        hi = x.astype(BF16)
        q2[h, :, 0:DIM] = hi
        q2[h, :, DIM : 2 * DIM] = (x - hi.astype(F32)).astype(BF16)
    mx[...] = jnp.full(mx.shape, -BIG, F32)
    acc[...] = jnp.zeros(acc.shape, F32)
    va[:, DIM : 2 * DIM] = jnp.ones((SPAN, DIM), BF16)

    def unpack(chunk):
        for g in range(2):
            rows = pl.ds(g * GROUP, GROUP)
            k = kvb[chunk, rows, 0:DIM].astype(F32) * meta[chunk, pl.ds(g, 1), :]
            k = k.T.astype(BF16)
            kt[0:DIM, g * GROUP : (g + 1) * GROUP] = k
            kt[DIM : 2 * DIM, g * GROUP : (g + 1) * GROUP] = k
            v = kvb[chunk, rows, DIM : 2 * DIM].astype(F32) * meta[chunk, pl.ds(2 + g, 1), :]
            va[rows, 0:DIM] = v.astype(BF16)

    def attend(h, penalty):
        s = jnp.dot(q2[h], kt[...], preferred_element_type=F32)
        if penalty is None:
            s = s + bias[...]
        m_old = mx[h]
        m_new, p = [], []
        for r in range(2):
            rows = slice(r * SPAN, (r + 1) * SPAN)
            a, b = s[rows, 0:128], s[rows, 128:256]
            top = jnp.max(jnp.maximum(a, b), axis=1, keepdims=True)
            if penalty is None:
                m = jnp.maximum(m_old[rows], top)
                off = m
            else:
                m = jnp.maximum(m_old[rows], top - penalty[r])
                off = m + penalty[r]
            m_new.append(m)
            p.append(jnp.concatenate([jnp.exp2(a - off), jnp.exp2(b - off)], axis=1).astype(BF16))
        m_new = jnp.concatenate(m_new, axis=0)
        alpha = jnp.exp2(m_old - m_new)
        add = jnp.dot(jnp.concatenate(p, axis=0), va[...], preferred_element_type=F32)
        numer = acc[h, :, 0:DIM] * alpha + add[:, 0:DIM]
        total = acc[h, :, DIM : 2 * DIM] * alpha + add[:, DIM : 2 * DIM]
        return m_new, numer, total

    def update(penalty):
        for h in range(HEADS):
            m_new, numer, total = attend(h, penalty)
            mx[h] = m_new
            acc[h, :, 0:DIM] = numer
            acc[h, :, DIM : 2 * DIM] = total

    def penalties(chunk):
        key = meta[chunk, pl.ds(4, 1), :]
        return [jnp.where(key < meta[r, pl.ds(4, 1), :], 0.0, BIG) for r in range(2)]

    for s in range(2):
        own[s].wait()

    def own_step(s, carry):
        unpack(s)
        row = lax.broadcasted_iota(jnp.int32, (SPAN, 128), 0)
        col = lax.broadcasted_iota(jnp.int32, (SPAN, 128), 1)
        for r in range(2):
            apart = meta[r, pl.ds(4, 1), :] - meta[s, pl.ds(4, 1), :]
            for c in range(2):
                ahead_by = (row - col - c * 128).astype(F32) + apart
                bias[r * SPAN : (r + 1) * SPAN, c * 128 : (c + 1) * 128] = jnp.where(ahead_by >= 0, 0.0, -BIG)
        update(None)
        return carry

    lax.fori_loop(0, 2, own_step, 0)

    def step(t, carry):
        arrived(t)
        for chunk, later in FORWARD.items():
            @pl.when(t == chunk)
            def _(chunk=chunk, later=later):
                send(kvb.at[chunk], meta.at[chunk], later, ahead)
        unpack(t)
        update(penalties(t))
        return carry

    lax.fori_loop(2, CHUNKS - 1, step, 0)

    last = CHUNKS - 1
    arrived(last)
    unpack(last)
    penalty = penalties(last)
    outs = []
    for h in range(HEADS):
        _, numer, total = attend(h, penalty)
        stage[h] = (numer / total).astype(BF16)
        outs.append(pltpu.make_async_copy(stage.at[h], out_hbm.at[:, pl.ds(h * DIM, DIM)], out_sem.at[h]))
        outs[h].start()
    for chunk in range(2, CHUNKS):
        sent(chunk)
    for copy in outs:
        copy.wait()


def solution(mesh):
    n_outer, n_inner = mesh.shape["outer"], mesh.shape["inner"]

    def local(queries, kv_codes, scale_exp, positions):
        tokens = queries.shape[0]
        anywhere = pl.BlockSpec(memory_space=pl.ANY)
        scalars = pl.BlockSpec(memory_space=pltpu.SMEM)
        return pl.pallas_call(
            functools.partial(kernel, n_outer, n_inner),
            out_shape=jax.ShapeDtypeStruct((tokens, HEADS * DIM), BF16),
            in_specs=[anywhere, anywhere, scalars, scalars],
            out_specs=anywhere,
            scratch_shapes=[
                pltpu.VMEM((tokens, HEADS * DIM), BF16),
                pltpu.VMEM((CHUNKS, SPAN, 2 * DIM), BF16),
                pltpu.VMEM((CHUNKS, 8, 128), F32),
                pltpu.VMEM((HEADS, tokens, 2 * DIM), BF16),
                pltpu.VMEM((2 * DIM, SPAN), BF16),
                pltpu.VMEM((SPAN, 2 * DIM), BF16),
                pltpu.VMEM((HEADS, tokens, 2 * DIM), F32),
                pltpu.VMEM((HEADS, tokens, 128), F32),
                pltpu.VMEM((tokens, SPAN), F32),
                pltpu.VMEM((HEADS, tokens, DIM), BF16),
                pltpu.SemaphoreType.DMA((3,)),
                pltpu.SemaphoreType.DMA((CHUNKS,)),
                pltpu.SemaphoreType.DMA((CHUNKS,)),
                pltpu.SemaphoreType.DMA((CHUNKS,)),
                pltpu.SemaphoreType.DMA((CHUNKS,)),
                pltpu.SemaphoreType.DMA((HEADS,)),
            ],
            compiler_params=pltpu.CompilerParams(
                collective_id=0, has_side_effects=True, vmem_limit_bytes=60 * 2**20
            ),
            name="span_attention",
        )(queries, kv_codes, scale_exp.T, positions)

    split = P(("outer", "inner"), None)
    return jax.shard_map(
        local,
        mesh=mesh,
        in_specs=(split, split, split, P(("outer", "inner"))),
        out_specs=split,
        check_vma=False,
    )
```

time: 106 us -> 47.6 us (0.45)
  the two profiles are of different devices: /device:TPU:6 before, /device:TPU:8 now
where the time goes in v1:
time: 47.6 us; the launch traced here: 47.4 us
  Pallas kernels  45.2 us (95%)
  local copies, waits for them, and re-layouts  2.26 us (5%)
    pallas_call x1, Pallas kernels, local(): pl.pallas_call(functools.partial(kernel, n_outer, n_inner), out_shape=jax...  45.2 us
    unnamed x1, local copies, waits for them, and re-layouts  2.26 us

profile of v1, /device:TPU:8, one launch (start us, length us, event | category | flops | bytes accessed | tf_op | source)
XLA Modules:
  0.0 47.4 jit_solution(14815131625223934728)
XLA Ops:
  0.0 45.2 %span_attention.1 = bf16[512,1024]{1,0:T(8,128)(2,1)} custom-call(bf16[512,1024]{1,0:T(8,128)(2,1)} %q_hbm.1, bf16[512,256]{1,0:T(8,128)(2,1)} %kv_hbm.1, s32[2,4]{1,0:T(2,128)} %bitcast.1, s32[512]{0:T(512)} %pos_ref.1), custom_call_target="tpu_custom_call" | custom-call | tf_op jit(solution)/shard_map/span_attention/pallas_call | solution.py:202
  45.2 2.3 %copy.6 = bf16[512,1024]{1,0:T(8,128)(2,1)} copy(bf16[512,1024]{1,0:T(8,128)(2,1)} %span_attention.1) | data formatting | bytes 2097152

commit v2 on v1

v2 whole, which is shorter than its diff:
```python
import functools
import math

import jax
import jax.numpy as jnp
from jax import lax
from jax.experimental import pallas as pl
from jax.experimental.pallas import tpu as pltpu
from jax.sharding import PartitionSpec as P

MESH = pl.DeviceIdType.MESH
HEADS = 8
DIM = 128
SPAN = 256
GROUP = 128
BIG = 1e30
SCALE = math.log2(math.e) / math.sqrt(128.0)
BF16 = jnp.bfloat16
F32 = jnp.float32

BLOCKS, CHUNKS = 5, 10


def kernel(
    n_outer, n_inner,
    q_hbm, kv_hbm, exp_hbm, pos_hbm, out_ref,
    exp_ref, pos_ref, q_in, kvb, notes, q2, kt, va, acc, mx, bias,
    local_sem, send_sem, recv_sem, note_send, note_recv,
):
    o, i = lax.axis_index("outer"), lax.axis_index("inner")
    z = lax.rem(i, 16)
    ahead = (o, lax.rem(i + 1, n_inner))
    behind = (o, lax.rem(i + n_inner - 1, n_inner))
    above = (lax.rem(o + 1, n_outer), i)
    below = (lax.rem(o + n_outer - 1, n_outer), i)

    barrier = pltpu.get_barrier_semaphore()
    for peer in (behind, below):
        pl.semaphore_signal(barrier, inc=1, device_id=peer, device_id_type=MESH)

    local = [
        pltpu.make_async_copy(exp_hbm, exp_ref, local_sem.at[0]),
        pltpu.make_async_copy(pos_hbm, pos_ref, local_sem.at[1]),
        pltpu.make_async_copy(kv_hbm.at[pl.ds(0, SPAN)], kvb.at[0], local_sem.at[2]),
        pltpu.make_async_copy(kv_hbm.at[pl.ds(SPAN, SPAN)], kvb.at[1], local_sem.at[3]),
        pltpu.make_async_copy(q_hbm, q_in, local_sem.at[4]),
    ]
    for part in local:
        part.start()

    def copy(src, dst, sent, arrived, device):
        return pltpu.make_async_remote_copy(
            src_ref=src, dst_ref=dst, send_sem=sent, recv_sem=arrived, device_id=device, device_id_type=MESH
        )

    def chunk_copy(src, chunk, device):
        return copy(src, kvb.at[chunk], send_sem.at[chunk], recv_sem.at[chunk], device)

    def note_copy(src, block, device):
        return copy(src, notes.at[block], note_send.at[block], note_recv.at[block], device)

    pl.semaphore_wait(barrier, 2)
    def send_own(s):
        rows = kv_hbm.at[pl.ds(s * SPAN, SPAN)]
        chunk_copy(rows, 4 + s, ahead).start()
        chunk_copy(rows, 2 + s, above).start()

    send_own(0)

    local[0].wait()
    local[1].wait()
    row = lax.broadcasted_iota(jnp.int32, (16, 128), 0)
    note = jnp.zeros((16, 128), F32)
    for side in range(2):
        for g in range(4):
            e = exp_ref[side, g]
            note = jnp.where(row == 4 * side + g, jnp.where(e > 0, 2.0, jnp.where(e < 0, 0.5, 1.0)), note)
    for s in range(2):
        index = lax.div(pos_ref[s * SPAN], SPAN)
        note = jnp.where(row == 8 + 2 * s, lax.div(index, 32).astype(F32), note)
        note = jnp.where(row == 9 + 2 * s, lax.rem(index, 32).astype(F32), note)
    notes[0] = note.astype(BF16)
    note_copy(notes.at[0], 2, ahead).start()
    note_copy(notes.at[0], 1, above).start()
    send_own(1)

    late = z < 3
    turns = {
        4: jnp.where(late, 4, 2),
        5: jnp.where(late, 5, 3),
        6: jnp.where(late, 6, 5),
        7: jnp.int32(7),
    }

    def arrive(chunk):
        chunk_copy(kvb.at[chunk], chunk, ahead).wait_recv()

    def exchange(t):
        for chunk, turn in turns.items():
            @pl.when(t == turn)
            def _(chunk=chunk):
                block = chunk // 2
                if chunk % 2 == 0:
                    note_copy(notes.at[block], block, ahead).wait_recv()
                    note_copy(notes.at[block], block + 1, ahead).start()
                arrive(chunk)
                chunk_copy(kvb.at[chunk], chunk + 2, ahead).start()

    local[4].wait()
    for h in range(HEADS):
        x = q_in[:, h * DIM : (h + 1) * DIM].astype(F32) * SCALE
        hi = x.astype(BF16)
        q2[h, :, 0:DIM] = hi
        q2[h, :, DIM : 2 * DIM] = (x - hi.astype(F32)).astype(BF16)
    mx[...] = jnp.full(mx.shape, -BIG, F32)
    acc[...] = jnp.zeros(acc.shape, F32)
    va[:, DIM : 2 * DIM] = jnp.ones((SPAN, DIM), BF16)

    def unpack(block, span):
        note = notes[block].astype(F32)

        def of(low, high):
            return jnp.where(span == 0, note[low : low + 1], note[high : high + 1])

        for g in range(2):
            rows = pl.ds(g * GROUP, GROUP)
            k = kvb[2 * block + span, rows, 0:DIM].astype(F32) * of(g, 2 + g)
            k = k.T.astype(BF16)
            kt[0:DIM, g * GROUP : (g + 1) * GROUP] = k
            kt[DIM : 2 * DIM, g * GROUP : (g + 1) * GROUP] = k
            v = kvb[2 * block + span, rows, DIM : 2 * DIM].astype(F32) * of(4 + g, 6 + g)
            va[rows, 0:DIM] = v.astype(BF16)
        return of(8, 10) * 32.0 + of(9, 11)

    def attend(h, penalty):
        s = jnp.dot(q2[h], kt[...], preferred_element_type=F32)
        if penalty is None:
            s = s + bias[...]
        m_old = mx[h]
        m_new, p = [], []
        for r in range(2):
            rows = slice(r * SPAN, (r + 1) * SPAN)
            a, b = s[rows, 0:128], s[rows, 128:256]
            top = jnp.max(jnp.maximum(a, b), axis=1, keepdims=True)
            if penalty is None:
                m = jnp.maximum(m_old[rows], top)
                off = m
            else:
                m = jnp.maximum(m_old[rows], top - penalty[r])
                off = m + penalty[r]
            m_new.append(m)
            p.append(jnp.concatenate([jnp.exp2(a - off), jnp.exp2(b - off)], axis=1).astype(BF16))
        m_new = jnp.concatenate(m_new, axis=0)
        alpha = jnp.exp2(m_old - m_new)
        add = jnp.dot(jnp.concatenate(p, axis=0), va[...], preferred_element_type=F32)
        numer = acc[h, :, 0:DIM] * alpha + add[:, 0:DIM]
        total = acc[h, :, DIM : 2 * DIM] * alpha + add[:, DIM : 2 * DIM]
        return m_new, numer, total

    def update(penalty):
        for h in range(HEADS):
            m_new, numer, total = attend(h, penalty)
            mx[h] = m_new
            acc[h, :, 0:DIM] = numer
            acc[h, :, DIM : 2 * DIM] = total

    note = notes[0].astype(F32)
    mine = [note[8 + 2 * r : 9 + 2 * r] * 32.0 + note[9 + 2 * r : 10 + 2 * r] for r in range(2)]

    def penalties(place):
        return [jnp.where(place < mine[r], 0.0, BIG) for r in range(2)]

    local[2].wait()
    local[3].wait()

    def own_step(s, carry):
        place = unpack(0, s)
        row = lax.broadcasted_iota(jnp.int32, (SPAN, 128), 0)
        col = lax.broadcasted_iota(jnp.int32, (SPAN, 128), 1)
        for r in range(2):
            apart = (mine[r] - place) * SPAN
            for c in range(2):
                beyond = (row - col - c * 128).astype(F32) + apart
                bias[r * SPAN : (r + 1) * SPAN, c * 128 : (c + 1) * 128] = jnp.where(beyond >= 0, 0.0, -BIG)
        update(None)
        return carry

    lax.fori_loop(0, 2, own_step, 0)

    def step(t, carry):
        exchange(t)

        @pl.when(jnp.logical_or(t == 2, t == 8))
        def _():
            block = t // 2
            note_copy(notes.at[block], block, ahead).wait_recv()

        @pl.when(jnp.logical_or(t < 4, t == 8))
        def _():
            arrive(t)

        update(penalties(unpack(t // 2, lax.rem(t, 2))))
        return carry

    lax.fori_loop(2, CHUNKS - 1, step, 0)

    arrive(CHUNKS - 1)
    penalty = penalties(unpack(BLOCKS - 1, 1))
    for h in range(HEADS):
        _, numer, total = attend(h, penalty)
        out_ref[:, h * DIM : (h + 1) * DIM] = (numer / total).astype(BF16)

    for chunk in range(2, CHUNKS):
        chunk_copy(kvb.at[chunk], chunk, ahead).wait_send()
    for block in range(1, BLOCKS):
        note_copy(notes.at[block], block, ahead).wait_send()


def solution(mesh):
    n_outer, n_inner = mesh.shape["outer"], mesh.shape["inner"]

    def local(queries, kv_codes, scale_exp, positions):
        tokens = queries.shape[0]
        in_hbm = pl.BlockSpec(memory_space=pltpu.HBM)
        operands = [queries, kv_codes, scale_exp.T, positions]
        return pl.pallas_call(
            functools.partial(kernel, n_outer, n_inner),
            out_shape=pltpu.VMEM((tokens, HEADS * DIM), BF16),
            in_specs=[in_hbm] * 4,
            out_specs=pl.BlockSpec(memory_space=pltpu.VMEM),
            scratch_shapes=[
                pltpu.SMEM((2, tokens // GROUP), jnp.int32),
                pltpu.SMEM((tokens,), jnp.int32),
                pltpu.VMEM((tokens, HEADS * DIM), BF16),
                pltpu.VMEM((CHUNKS, SPAN, 2 * DIM), BF16),
                pltpu.VMEM((BLOCKS, 16, 128), BF16),
                pltpu.VMEM((HEADS, tokens, 2 * DIM), BF16),
                pltpu.VMEM((2 * DIM, SPAN), BF16),
                pltpu.VMEM((SPAN, 2 * DIM), BF16),
                pltpu.VMEM((HEADS, tokens, 2 * DIM), F32),
                pltpu.VMEM((HEADS, tokens, 128), F32),
                pltpu.VMEM((tokens, SPAN), F32),
                pltpu.SemaphoreType.DMA((5,)),
                pltpu.SemaphoreType.DMA((CHUNKS,)),
                pltpu.SemaphoreType.DMA((CHUNKS,)),
                pltpu.SemaphoreType.DMA((BLOCKS,)),
                pltpu.SemaphoreType.DMA((BLOCKS,)),
            ],
            compiler_params=pltpu.CompilerParams(
                collective_id=0, has_side_effects=True, vmem_limit_bytes=40 * 2**20
            ),
            name="span_attention",
        )(*[pltpu.with_memory_space_constraint(x, pltpu.HBM) for x in operands])

    split = P(("outer", "inner"), None)
    return jax.shard_map(
        local,
        mesh=mesh,
        in_specs=(split, split, split, P(("outer", "inner"))),
        out_specs=split,
        check_vma=False,
    )
```

time: 47.6 us -> 35.4 us (0.74)
  the two profiles are of different devices: /device:TPU:8 before, /device:TPU:6 now
where the time goes in v2:
time: 35.4 us; the launch traced here: 35.2 us
  Pallas kernels  34.2 us (97%)
  local copies, waits for them, and re-layouts  0.97 us (3%)
    pallas_call x1, Pallas kernels, local(): pl.pallas_call(functools.partial(kernel, n_outer, n_inner), out_shape=plt...  34.2 us
    unnamed x1, local copies, waits for them, and re-layouts  0.97 us

profile of v2, /device:TPU:6, one launch (start us, length us, event | category | flops | bytes accessed | tf_op | source)
XLA Modules:
  0.0 35.2 jit_solution(10762045212547455401)
XLA Ops:
  0.0 34.2 %span_attention.1 = bf16[512,1024]{1,0:T(8,128)(2,1)S(1)} custom-call(bf16[512,1024]{1,0:T(8,128)(2,1)} %q_hbm.1, bf16[512,256]{1,0:T(8,128)(2,1)} %kv_hbm.1, s32[2,4]{1,0:T(2,128)} %bitcast.1, s32[512]{0:T(512)} %pos_hbm.1), custom_call_target="tpu_custom_call" | custom-call | tf_op jit(solution)/shard_map/span_attention/pallas_call | solution.py:226
  34.3 1.0 %copy.6 = bf16[512,1024]{1,0:T(8,128)(2,1)} copy(bf16[512,1024]{1,0:T(8,128)(2,1)S(1)} %span_attention.1) | data formatting | bytes 2097152

commit v3 on v2

--- a/solution.py
+++ b/solution.py
@@ -24,7 +24,7 @@
 def kernel(
     n_outer, n_inner,
     q_hbm, kv_hbm, exp_hbm, pos_hbm, out_ref,
-    exp_ref, pos_ref, q_in, kvb, notes, q2, kt, va, acc, mx, bias,
+    exp_ref, pos_ref, q_in, kvb, notes, q2, kt, va, acc, mx, bias, weights,
     local_sem, send_sem, recv_sem, note_send, note_recv,
 ):
     o, i = lax.axis_index("outer"), lax.axis_index("inner")
@@ -55,6 +55,11 @@
 
     def chunk_copy(src, chunk, device):
         return copy(src, kvb.at[chunk], send_sem.at[chunk], recv_sem.at[chunk], device)
+
+    def half_copy(src, side, device):
+        half = pl.ds(side * DIM, DIM)
+        sem = CHUNKS - 1 + side
+        return copy(src.at[:, half], kvb.at[CHUNKS - 1, :, half], send_sem.at[sem], recv_sem.at[sem], device)
 
     def note_copy(src, block, device):
         return copy(src, notes.at[block], note_send.at[block], note_recv.at[block], device)
@@ -104,7 +109,11 @@
                     note_copy(notes.at[block], block, ahead).wait_recv()
                     note_copy(notes.at[block], block + 1, ahead).start()
                 arrive(chunk)
-                chunk_copy(kvb.at[chunk], chunk + 2, ahead).start()
+                if chunk + 2 < CHUNKS - 1:
+                    chunk_copy(kvb.at[chunk], chunk + 2, ahead).start()
+                else:
+                    for side in range(2):
+                        half_copy(kvb.at[chunk], side, ahead).start()
 
     local[4].wait()
     for h in range(HEADS):
@@ -116,7 +125,7 @@
     acc[...] = jnp.zeros(acc.shape, F32)
     va[:, DIM : 2 * DIM] = jnp.ones((SPAN, DIM), BF16)
 
-    def unpack(block, span):
+    def unpack(block, span, sides=(0, 1)):
         note = notes[block].astype(F32)
 
         def of(low, high):
@@ -124,15 +133,17 @@
 
         for g in range(2):
             rows = pl.ds(g * GROUP, GROUP)
-            k = kvb[2 * block + span, rows, 0:DIM].astype(F32) * of(g, 2 + g)
-            k = k.T.astype(BF16)
-            kt[0:DIM, g * GROUP : (g + 1) * GROUP] = k
-            kt[DIM : 2 * DIM, g * GROUP : (g + 1) * GROUP] = k
-            v = kvb[2 * block + span, rows, DIM : 2 * DIM].astype(F32) * of(4 + g, 6 + g)
-            va[rows, 0:DIM] = v.astype(BF16)
+            if 0 in sides:
+                k = kvb[2 * block + span, rows, 0:DIM].astype(F32) * of(g, 2 + g)
+                k = k.T.astype(BF16)
+                kt[0:DIM, g * GROUP : (g + 1) * GROUP] = k
+                kt[DIM : 2 * DIM, g * GROUP : (g + 1) * GROUP] = k
+            if 1 in sides:
+                v = kvb[2 * block + span, rows, DIM : 2 * DIM].astype(F32) * of(4 + g, 6 + g)
+                va[rows, 0:DIM] = v.astype(BF16)
         return of(8, 10) * 32.0 + of(9, 11)
 
-    def attend(h, penalty):
+    def weigh(h, penalty):
         s = jnp.dot(q2[h], kt[...], preferred_element_type=F32)
         if penalty is None:
             s = s + bias[...]
@@ -151,15 +162,18 @@
             m_new.append(m)
             p.append(jnp.concatenate([jnp.exp2(a - off), jnp.exp2(b - off)], axis=1).astype(BF16))
         m_new = jnp.concatenate(m_new, axis=0)
-        alpha = jnp.exp2(m_old - m_new)
-        add = jnp.dot(jnp.concatenate(p, axis=0), va[...], preferred_element_type=F32)
+        return m_new, jnp.exp2(m_old - m_new), jnp.concatenate(p, axis=0)
+
+    def gather(h, alpha, p):
+        add = jnp.dot(p, va[...], preferred_element_type=F32)
         numer = acc[h, :, 0:DIM] * alpha + add[:, 0:DIM]
         total = acc[h, :, DIM : 2 * DIM] * alpha + add[:, DIM : 2 * DIM]
-        return m_new, numer, total
+        return numer, total
 
     def update(penalty):
         for h in range(HEADS):
-            m_new, numer, total = attend(h, penalty)
+            m_new, alpha, p = weigh(h, penalty)
+            numer, total = gather(h, alpha, p)
             mx[h] = m_new
             acc[h, :, 0:DIM] = numer
             acc[h, :, DIM : 2 * DIM] = total
@@ -204,14 +218,22 @@
 
     lax.fori_loop(2, CHUNKS - 1, step, 0)
 
-    arrive(CHUNKS - 1)
-    penalty = penalties(unpack(BLOCKS - 1, 1))
+    half_copy(kvb.at[CHUNKS - 1], 0, ahead).wait_recv()
+    penalty = penalties(unpack(BLOCKS - 1, 1, (0,)))
     for h in range(HEADS):
-        _, numer, total = attend(h, penalty)
+        _, alpha, p = weigh(h, penalty)
+        mx[h] = alpha
+        weights[h] = p
+    half_copy(kvb.at[CHUNKS - 1], 1, ahead).wait_recv()
+    unpack(BLOCKS - 1, 1, (1,))
+    for h in range(HEADS):
+        numer, total = gather(h, mx[h], weights[h])
         out_ref[:, h * DIM : (h + 1) * DIM] = (numer / total).astype(BF16)
 
-    for chunk in range(2, CHUNKS):
+    for chunk in range(2, CHUNKS - 1):
         chunk_copy(kvb.at[chunk], chunk, ahead).wait_send()
+    for side in range(2):
+        half_copy(kvb.at[CHUNKS - 1], side, ahead).wait_send()
     for block in range(1, BLOCKS):
         note_copy(notes.at[block], block, ahead).wait_send()
 
@@ -240,9 +262,10 @@
                 pltpu.VMEM((HEADS, tokens, 2 * DIM), F32),
                 pltpu.VMEM((HEADS, tokens, 128), F32),
                 pltpu.VMEM((tokens, SPAN), F32),
+                pltpu.VMEM((HEADS, tokens, SPAN), BF16),
                 pltpu.SemaphoreType.DMA((5,)),
-                pltpu.SemaphoreType.DMA((CHUNKS,)),
-                pltpu.SemaphoreType.DMA((CHUNKS,)),
+                pltpu.SemaphoreType.DMA((CHUNKS + 1,)),
+                pltpu.SemaphoreType.DMA((CHUNKS + 1,)),
                 pltpu.SemaphoreType.DMA((BLOCKS,)),
                 pltpu.SemaphoreType.DMA((BLOCKS,)),
             ],

time: 35.4 us -> 35.1 us (level)
  no operation moved by 1% of the time
where the time goes in v3:
time: 35.1 us; the launch traced here: 34.9 us
  Pallas kernels  33.9 us (97%)
  local copies, waits for them, and re-layouts  0.97 us (3%)
    pallas_call x1, Pallas kernels, local(): pl.pallas_call(functools.partial(kernel, n_outer, n_inner), out_shape=plt...  33.9 us
    unnamed x1, local copies, waits for them, and re-layouts  0.97 us

profile of v3, /device:TPU:6, one launch (start us, length us, event | category | flops | bytes accessed | tf_op | source)
XLA Modules:
  0.0 34.9 jit_solution(13873423225154281158)
XLA Ops:
  0.0 33.9 %span_attention.1 = bf16[512,1024]{1,0:T(8,128)(2,1)S(1)} custom-call(bf16[512,1024]{1,0:T(8,128)(2,1)} %q_hbm.1, bf16[512,256]{1,0:T(8,128)(2,1)} %kv_hbm.1, s32[2,4]{1,0:T(2,128)} %bitcast.1, s32[512]{0:T(512)} %pos_hbm.1), custom_call_target="tpu_custom_call" | custom-call | tf_op jit(solution)/shard_map/span_attention/pallas_call | solution.py:248
  34.0 1.0 %copy.6 = bf16[512,1024]{1,0:T(8,128)(2,1)} copy(bf16[512,1024]{1,0:T(8,128)(2,1)S(1)} %span_attention.1) | data formatting | bytes 2097152

commit v4 on v3

--- a/solution.py
+++ b/solution.py
@@ -19,13 +19,34 @@
 F32 = jnp.float32
 
 BLOCKS, CHUNKS = 5, 10
+LAST_Z, FAR_Z, MID_Z = 15, 13, 6
+MID_TURN = 6
+SIDES = (0, 1)
+
+
+def gather(acc, va, h, alpha, p):
+    add = jnp.dot(p, va[...], preferred_element_type=F32)
+    numer = acc[h, :, 0:DIM] * alpha + add[:, 0:DIM]
+    total = acc[h, :, DIM : 2 * DIM] * alpha + add[:, DIM : 2 * DIM]
+    return numer, total
+
+
+def finish(acc, alpha, weights, va, out_hbm, stage, sem):
+    outs = []
+    for h in range(HEADS):
+        numer, total = gather(acc, va, h, alpha[h], weights[h])
+        stage[h] = (numer / total).astype(BF16)
+        outs.append(pltpu.make_async_copy(stage.at[h], out_hbm.at[:, pl.ds(h * DIM, DIM)], sem.at[h]))
+        outs[h].start()
+    for out in outs:
+        out.wait()
 
 
 def kernel(
     n_outer, n_inner,
-    q_hbm, kv_hbm, exp_hbm, pos_hbm, out_ref,
-    exp_ref, pos_ref, q_in, kvb, notes, q2, kt, va, acc, mx, bias, weights,
-    local_sem, send_sem, recv_sem, note_send, note_recv,
+    q_hbm, kv_hbm, exp_hbm, pos_hbm, acc, mx, weights, va,
+    exp_ref, pos_ref, q_in, kvb, notes, relay, q2, kt, bias,
+    local_sem, send_sem, recv_sem, note_send, note_recv, far_send, far_recv, mid_send,
 ):
     o, i = lax.axis_index("outer"), lax.axis_index("inner")
     z = lax.rem(i, 16)
@@ -36,6 +57,22 @@
 
     barrier = pltpu.get_barrier_semaphore()
     for peer in (behind, below):
+        pl.semaphore_signal(barrier, inc=1, device_id=peer, device_id_type=MESH)
+
+    def at(i):
+        return (o, lax.rem(i + n_inner, n_inner))
+
+    core_1 = lax.rem(o, 2) == 1
+    far, mid = jnp.logical_and(core_1, z == FAR_Z), jnp.logical_and(core_1, z == MID_Z)
+    first, last = jnp.logical_and(core_1, z == 0), jnp.logical_and(core_1, z == LAST_Z)
+
+    @pl.when(first)
+    def _():
+        pl.semaphore_signal(barrier, inc=1, device_id=at(i + MID_Z), device_id_type=MESH)
+
+    @pl.when(mid)
+    def _():
+        peer = at(i + 16 + FAR_Z - MID_Z)
         pl.semaphore_signal(barrier, inc=1, device_id=peer, device_id_type=MESH)
 
     local = [
@@ -64,7 +101,29 @@
     def note_copy(src, block, device):
         return copy(src, notes.at[block], note_send.at[block], note_recv.at[block], device)
 
-    pl.semaphore_wait(barrier, 2)
+    def to_relay(side, device):
+        src = kv_hbm.at[pl.ds(SPAN, SPAN), pl.ds(side * DIM, DIM)]
+        return copy(src, relay.at[side], far_send.at[side], far_recv.at[side], device)
+
+    def from_relay(side, device):
+        dst = kvb.at[CHUNKS - 1, :, pl.ds(side * DIM, DIM)]
+        return copy(relay.at[side], dst, mid_send.at[side], recv_sem.at[CHUNKS - 1 + side], device)
+
+    relays = jnp.logical_or(far, mid)
+
+    @pl.when(relays)
+    def _():
+        pl.semaphore_wait(barrier, 3)
+
+    @pl.when(jnp.logical_not(relays))
+    def _():
+        pl.semaphore_wait(barrier, 2)
+
+    @pl.when(far)
+    def _():
+        for side in SIDES:
+            to_relay(side, at(i + 16 - FAR_Z + MID_Z)).start()
+
     def send_own(s):
         rows = kv_hbm.at[pl.ds(s * SPAN, SPAN)]
         chunk_copy(rows, 4 + s, ahead).start()
@@ -94,13 +153,19 @@
         4: jnp.where(late, 4, 2),
         5: jnp.where(late, 5, 3),
         6: jnp.where(late, 6, 5),
-        7: jnp.int32(7),
+        7: jnp.where(z > 10, 6, 7),
     }
 
     def arrive(chunk):
         chunk_copy(kvb.at[chunk], chunk, ahead).wait_recv()
 
     def exchange(t):
+        @pl.when(jnp.logical_and(mid, t == MID_TURN))
+        def _():
+            for side in SIDES:
+                to_relay(side, ahead).wait_recv()
+                from_relay(side, at(i - MID_Z)).start()
+
         for chunk, turn in turns.items():
             @pl.when(t == turn)
             def _(chunk=chunk):
@@ -113,7 +178,9 @@
                     chunk_copy(kvb.at[chunk], chunk + 2, ahead).start()
                 else:
                     for side in range(2):
-                        half_copy(kvb.at[chunk], side, ahead).start()
+                        @pl.when(jnp.logical_not(last) if side in SIDES else z >= 0)
+                        def _(side=side):
+                            half_copy(kvb.at[chunk], side, ahead).start()
 
     local[4].wait()
     for h in range(HEADS):
@@ -164,16 +231,10 @@
         m_new = jnp.concatenate(m_new, axis=0)
         return m_new, jnp.exp2(m_old - m_new), jnp.concatenate(p, axis=0)
 
-    def gather(h, alpha, p):
-        add = jnp.dot(p, va[...], preferred_element_type=F32)
-        numer = acc[h, :, 0:DIM] * alpha + add[:, 0:DIM]
-        total = acc[h, :, DIM : 2 * DIM] * alpha + add[:, DIM : 2 * DIM]
-        return numer, total
-
     def update(penalty):
         for h in range(HEADS):
             m_new, alpha, p = weigh(h, penalty)
-            numer, total = gather(h, alpha, p)
+            numer, total = gather(acc, va, h, alpha, p)
             mx[h] = m_new
             acc[h, :, 0:DIM] = numer
             acc[h, :, DIM : 2 * DIM] = total
@@ -226,14 +287,24 @@
         weights[h] = p
     half_copy(kvb.at[CHUNKS - 1], 1, ahead).wait_recv()
     unpack(BLOCKS - 1, 1, (1,))
-    for h in range(HEADS):
-        numer, total = gather(h, mx[h], weights[h])
-        out_ref[:, h * DIM : (h + 1) * DIM] = (numer / total).astype(BF16)
 
     for chunk in range(2, CHUNKS - 1):
         chunk_copy(kvb.at[chunk], chunk, ahead).wait_send()
     for side in range(2):
-        half_copy(kvb.at[CHUNKS - 1], side, ahead).wait_send()
+        @pl.when(jnp.logical_not(last) if side in SIDES else z >= 0)
+        def _(side=side):
+            half_copy(kvb.at[CHUNKS - 1], side, ahead).wait_send()
+
+    @pl.when(far)
+    def _():
+        for side in SIDES:
+            to_relay(side, ahead).wait_send()
+
+    @pl.when(mid)
+    def _():
+        for side in SIDES:
+            from_relay(side, ahead).wait_send()
+
     for block in range(1, BLOCKS):
         note_copy(notes.at[block], block, ahead).wait_send()
 
@@ -245,35 +316,53 @@
         tokens = queries.shape[0]
         in_hbm = pl.BlockSpec(memory_space=pltpu.HBM)
         operands = [queries, kv_codes, scale_exp.T, positions]
-        return pl.pallas_call(
+        in_vmem = pl.BlockSpec(memory_space=pltpu.VMEM)
+        state = pl.pallas_call(
             functools.partial(kernel, n_outer, n_inner),
-            out_shape=pltpu.VMEM((tokens, HEADS * DIM), BF16),
+            out_shape=[
+                pltpu.VMEM((HEADS, tokens, 2 * DIM), F32),
+                pltpu.VMEM((HEADS, tokens, 128), F32),
+                pltpu.VMEM((HEADS, tokens, SPAN), BF16),
+                pltpu.VMEM((SPAN, 2 * DIM), BF16),
+            ],
             in_specs=[in_hbm] * 4,
-            out_specs=pl.BlockSpec(memory_space=pltpu.VMEM),
+            out_specs=[in_vmem] * 4,
             scratch_shapes=[
                 pltpu.SMEM((2, tokens // GROUP), jnp.int32),
                 pltpu.SMEM((tokens,), jnp.int32),
                 pltpu.VMEM((tokens, HEADS * DIM), BF16),
                 pltpu.VMEM((CHUNKS, SPAN, 2 * DIM), BF16),
                 pltpu.VMEM((BLOCKS, 16, 128), BF16),
+                pltpu.VMEM((2, SPAN, DIM), BF16),
                 pltpu.VMEM((HEADS, tokens, 2 * DIM), BF16),
                 pltpu.VMEM((2 * DIM, SPAN), BF16),
-                pltpu.VMEM((SPAN, 2 * DIM), BF16),
-                pltpu.VMEM((HEADS, tokens, 2 * DIM), F32),
-                pltpu.VMEM((HEADS, tokens, 128), F32),
                 pltpu.VMEM((tokens, SPAN), F32),
-                pltpu.VMEM((HEADS, tokens, SPAN), BF16),
                 pltpu.SemaphoreType.DMA((5,)),
                 pltpu.SemaphoreType.DMA((CHUNKS + 1,)),
                 pltpu.SemaphoreType.DMA((CHUNKS + 1,)),
                 pltpu.SemaphoreType.DMA((BLOCKS,)),
                 pltpu.SemaphoreType.DMA((BLOCKS,)),
+                pltpu.SemaphoreType.DMA((2,)),
+                pltpu.SemaphoreType.DMA((2,)),
+                pltpu.SemaphoreType.DMA((2,)),
             ],
             compiler_params=pltpu.CompilerParams(
-                collective_id=0, has_side_effects=True, vmem_limit_bytes=40 * 2**20
+                collective_id=0, has_side_effects=True, vmem_limit_bytes=32 * 2**20
             ),
             name="span_attention",
         )(*[pltpu.with_memory_space_constraint(x, pltpu.HBM) for x in operands])
+        return pl.pallas_call(
+            finish,
+            out_shape=pltpu.HBM((tokens, HEADS * DIM), BF16),
+            in_specs=[in_vmem] * 4,
+            out_specs=in_hbm,
+            scratch_shapes=[
+                pltpu.VMEM((HEADS, tokens, DIM), BF16),
+                pltpu.SemaphoreType.DMA((HEADS,)),
+            ],
+            compiler_params=pltpu.CompilerParams(vmem_limit_bytes=24 * 2**20),
+            name="last_values",
+        )(*state)
 
     split = P(("outer", "inner"), None)
     return jax.shard_map(

time: 35.1 us -> 34.3 us (0.977)
  local copies, waits for them, and re-layouts: 0.97 us -> 0 us
    unnamed x1 -> x0, local copies, waits for them, and re-layouts: 0.97 us -> none
    pallas_call x1 -> x2, Pallas kernels: 33.9 us -> 33.9 us  [the longest x1 32.4 us: local(): pl.pallas_call(functools.partial(kernel, n_outer, n_inner), out_shape=[pl...]
where the time goes in v4:
time: 34.3 us; the launch traced here: 33.9 us
  Pallas kernels  33.9 us (99%)
    pallas_call x1, Pallas kernels, local(): pl.pallas_call(functools.partial(kernel, n_outer, n_inner), out_shape=[pl...  32.4 us
    pallas_call x1, Pallas kernels, local(): pl.pallas_call(finish, out_shape=pltpu.HBM((tokens, HEADS * DIM), BF16),...  1.51 us

profile of v4, /device:TPU:6, one launch (start us, length us, event | category | flops | bytes accessed | tf_op | source)
XLA Modules:
  0.0 33.9 jit_solution(10052820767610104597)
XLA Ops:
  0.0 32.4 %span_attention.1 = (f32[8,512,256]{2,1,0:T(8,128)S(1)}, f32[8,512,128]{2,1,0:T(8,128)S(1)}, bf16[8,512,256]{2,1,0:T(8,128)(2,1)S(1)}, bf16[256,256]{1,0:T(8,128)(2,1)S(1)}) custom-call(bf16[512,1024]{1,0:T(8,128)(2,1)} %q_hbm.1, bf16[512,256]{1,0:T(8,128)(2,1)} %kv_hbm.1, s32[2,4]{1,0:T(2,128)} %bitcast.1, s32[512]{0:T(512)} %pos_hbm.1), custom_call_target="tpu_custom_call" | custom-call | tf_op jit(solution)/shard_map/span_attention/pallas_call | solution.py:320
  32.4 1.5 %last_values.1 = bf16[512,1024]{1,0:T(8,128)(2,1)} custom-call(f32[8,512,256]{2,1,0:T(8,128)S(1)} %get-tuple-element.9.acc, f32[8,512,128]{2,1,0:T(8,128)S(1)} %get-tuple-element.10.alpha, bf16[8,512,256]{2,1,0:T(8,128)(2,1)S(1)} %get-tuple-element.11.weights, bf16[256,256]{1,0:T(8,128)(2,1)S(1)} %get-tuple-element.12.va), custom_call_target="tpu_custom_call" | custom-call | tf_op jit(solution)/shard_map/last_values/pallas_call | solution.py:354

commit v5 on v4

--- a/solution.py
+++ b/solution.py
@@ -20,8 +20,7 @@
 
 BLOCKS, CHUNKS = 5, 10
 LAST_Z, FAR_Z, MID_Z = 15, 13, 6
-MID_TURN = 6
-SIDES = (0, 1)
+PIECES, MID_TURNS = (2, 0, 1), {2: 6, 0: 7, 1: 7}
 
 
 def gather(acc, va, h, alpha, p):
@@ -101,13 +100,18 @@
     def note_copy(src, block, device):
         return copy(src, notes.at[block], note_send.at[block], note_recv.at[block], device)
 
-    def to_relay(side, device):
-        src = kv_hbm.at[pl.ds(SPAN, SPAN), pl.ds(side * DIM, DIM)]
-        return copy(src, relay.at[side], far_send.at[side], far_recv.at[side], device)
-
-    def from_relay(side, device):
-        dst = kvb.at[CHUNKS - 1, :, pl.ds(side * DIM, DIM)]
-        return copy(relay.at[side], dst, mid_send.at[side], recv_sem.at[CHUNKS - 1 + side], device)
+    def lanes(piece):
+        return pl.ds(0, 2 * DIM) if piece == 2 else pl.ds(piece * DIM, DIM)
+
+    def to_relay(piece, device):
+        src = kv_hbm.at[pl.ds(0 if piece == 2 else SPAN, SPAN), lanes(piece)]
+        dst = relay.at[1 if piece == 2 else 0, :, lanes(piece)]
+        return copy(src, dst, far_send.at[piece], far_recv.at[piece], device)
+
+    def from_relay(piece, device):
+        src = relay.at[1 if piece == 2 else 0, :, lanes(piece)]
+        chunk, sem = (CHUNKS - 2, CHUNKS - 2) if piece == 2 else (CHUNKS - 1, CHUNKS - 1 + piece)
+        return copy(src, kvb.at[chunk, :, lanes(piece)], mid_send.at[piece], recv_sem.at[sem], device)
 
     relays = jnp.logical_or(far, mid)
 
@@ -121,8 +125,8 @@
 
     @pl.when(far)
     def _():
-        for side in SIDES:
-            to_relay(side, at(i + 16 - FAR_Z + MID_Z)).start()
+        for piece in PIECES:
+            to_relay(piece, at(i + 16 - FAR_Z + MID_Z)).start()
 
     def send_own(s):
         rows = kv_hbm.at[pl.ds(s * SPAN, SPAN)]
@@ -160,11 +164,11 @@
         chunk_copy(kvb.at[chunk], chunk, ahead).wait_recv()
 
     def exchange(t):
-        @pl.when(jnp.logical_and(mid, t == MID_TURN))
-        def _():
-            for side in SIDES:
-                to_relay(side, ahead).wait_recv()
-                from_relay(side, at(i - MID_Z)).start()
+        for piece in PIECES:
+            @pl.when(jnp.logical_and(mid, t == MID_TURNS[piece]))
+            def _(piece=piece):
+                to_relay(piece, ahead).wait_recv()
+                from_relay(piece, at(i - MID_Z)).start()
 
         for chunk, turn in turns.items():
             @pl.when(t == turn)
@@ -174,13 +178,16 @@
                     note_copy(notes.at[block], block, ahead).wait_recv()
                     note_copy(notes.at[block], block + 1, ahead).start()
                 arrive(chunk)
-                if chunk + 2 < CHUNKS - 1:
+                if chunk < 6:
                     chunk_copy(kvb.at[chunk], chunk + 2, ahead).start()
                 else:
-                    for side in range(2):
-                        @pl.when(jnp.logical_not(last) if side in SIDES else z >= 0)
-                        def _(side=side):
-                            half_copy(kvb.at[chunk], side, ahead).start()
+                    @pl.when(jnp.logical_not(last))
+                    def _():
+                        if chunk == 6:
+                            chunk_copy(kvb.at[chunk], chunk + 2, ahead).start()
+                        else:
+                            for side in range(2):
+                                half_copy(kvb.at[chunk], side, ahead).start()
 
     local[4].wait()
     for h in range(HEADS):
@@ -288,22 +295,24 @@
     half_copy(kvb.at[CHUNKS - 1], 1, ahead).wait_recv()
     unpack(BLOCKS - 1, 1, (1,))
 
-    for chunk in range(2, CHUNKS - 1):
+    for chunk in range(2, CHUNKS - 2):
         chunk_copy(kvb.at[chunk], chunk, ahead).wait_send()
-    for side in range(2):
-        @pl.when(jnp.logical_not(last) if side in SIDES else z >= 0)
-        def _(side=side):
+
+    @pl.when(jnp.logical_not(last))
+    def _():
+        chunk_copy(kvb.at[CHUNKS - 2], CHUNKS - 2, ahead).wait_send()
+        for side in range(2):
             half_copy(kvb.at[CHUNKS - 1], side, ahead).wait_send()
 
     @pl.when(far)
     def _():
-        for side in SIDES:
-            to_relay(side, ahead).wait_send()
+        for piece in PIECES:
+            to_relay(piece, ahead).wait_send()
 
     @pl.when(mid)
     def _():
-        for side in SIDES:
-            from_relay(side, ahead).wait_send()
+        for piece in PIECES:
+            from_relay(piece, ahead).wait_send()
 
     for block in range(1, BLOCKS):
         note_copy(notes.at[block], block, ahead).wait_send()
@@ -333,7 +342,7 @@
                 pltpu.VMEM((tokens, HEADS * DIM), BF16),
                 pltpu.VMEM((CHUNKS, SPAN, 2 * DIM), BF16),
                 pltpu.VMEM((BLOCKS, 16, 128), BF16),
-                pltpu.VMEM((2, SPAN, DIM), BF16),
+                pltpu.VMEM((2, SPAN, 2 * DIM), BF16),
                 pltpu.VMEM((HEADS, tokens, 2 * DIM), BF16),
                 pltpu.VMEM((2 * DIM, SPAN), BF16),
                 pltpu.VMEM((tokens, SPAN), F32),
@@ -342,9 +351,9 @@
                 pltpu.SemaphoreType.DMA((CHUNKS + 1,)),
                 pltpu.SemaphoreType.DMA((BLOCKS,)),
                 pltpu.SemaphoreType.DMA((BLOCKS,)),
-                pltpu.SemaphoreType.DMA((2,)),
-                pltpu.SemaphoreType.DMA((2,)),
-                pltpu.SemaphoreType.DMA((2,)),
+                pltpu.SemaphoreType.DMA((3,)),
+                pltpu.SemaphoreType.DMA((3,)),
+                pltpu.SemaphoreType.DMA((3,)),
             ],
             compiler_params=pltpu.CompilerParams(
                 collective_id=0, has_side_effects=True, vmem_limit_bytes=32 * 2**20

time: 34.3 us -> 33.5 us (0.977)
  Pallas kernels: 33.9 us -> 33.3 us
    pallas_call x1, Pallas kernels: 32.4 us -> 31.8 us  [local(): pl.pallas_call(functools.partial(kernel, n_outer, n_inner), out_shape=[pl...]
where the time goes in v5:
time: 33.5 us; the launch traced here: 33.4 us
  Pallas kernels  33.3 us (99%)
    pallas_call x1, Pallas kernels, local(): pl.pallas_call(functools.partial(kernel, n_outer, n_inner), out_shape=[pl...  31.8 us
    pallas_call x1, Pallas kernels, local(): pl.pallas_call(finish, out_shape=pltpu.HBM((tokens, HEADS * DIM), BF16),...  1.51 us

profile of v5, /device:TPU:6, one launch (start us, length us, event | category | flops | bytes accessed | tf_op | source)
XLA Modules:
  0.0 33.4 jit_solution(10292914146282634112)
XLA Ops:
  0.0 31.8 %span_attention.1 = (f32[8,512,256]{2,1,0:T(8,128)S(1)}, f32[8,512,128]{2,1,0:T(8,128)S(1)}, bf16[8,512,256]{2,1,0:T(8,128)(2,1)S(1)}, bf16[256,256]{1,0:T(8,128)(2,1)S(1)}) custom-call(bf16[512,1024]{1,0:T(8,128)(2,1)} %q_hbm.1, bf16[512,256]{1,0:T(8,128)(2,1)} %kv_hbm.1, s32[2,4]{1,0:T(2,128)} %bitcast.1, s32[512]{0:T(512)} %pos_hbm.1), custom_call_target="tpu_custom_call" | custom-call | tf_op jit(solution)/shard_map/span_attention/pallas_call | solution.py:329
  31.8 1.5 %last_values.1 = bf16[512,1024]{1,0:T(8,128)(2,1)} custom-call(f32[8,512,256]{2,1,0:T(8,128)S(1)} %get-tuple-element.9.acc, f32[8,512,128]{2,1,0:T(8,128)S(1)} %get-tuple-element.10.alpha, bf16[8,512,256]{2,1,0:T(8,128)(2,1)S(1)} %get-tuple-element.11.weights, bf16[256,256]{1,0:T(8,128)(2,1)S(1)} %get-tuple-element.12.va), custom_call_target="tpu_custom_call" | custom-call | tf_op jit(solution)/shard_map/last_values/pallas_call | solution.py:363

commit v6 on v5

--- a/solution.py
+++ b/solution.py
@@ -20,7 +20,7 @@
 
 BLOCKS, CHUNKS = 5, 10
 LAST_Z, FAR_Z, MID_Z = 15, 13, 6
-PIECES, MID_TURNS = (2, 0, 1), {2: 6, 0: 7, 1: 7}
+PIECES, MID_TURNS = (2, 0, 1), {2: 5, 0: 6, 1: 6}
 
 
 def gather(acc, va, h, alpha, p):

time: 33.5 us -> 33.5 us (level)
  no operation moved by 1% of the time
where the time goes in v6:
time: 33.5 us; the launch traced here: 33.4 us
  Pallas kernels  33.3 us (99%)
    pallas_call x1, Pallas kernels, local(): pl.pallas_call(functools.partial(kernel, n_outer, n_inner), out_shape=[pl...  31.8 us
    pallas_call x1, Pallas kernels, local(): pl.pallas_call(finish, out_shape=pltpu.HBM((tokens, HEADS * DIM), BF16),...  1.51 us

profile of v6, /device:TPU:6, one launch (start us, length us, event | category | flops | bytes accessed | tf_op | source)
XLA Modules:
  0.0 33.4 jit_solution(9151482058360147734)
XLA Ops:
  0.0 31.8 %span_attention.1 = (f32[8,512,256]{2,1,0:T(8,128)S(1)}, f32[8,512,128]{2,1,0:T(8,128)S(1)}, bf16[8,512,256]{2,1,0:T(8,128)(2,1)S(1)}, bf16[256,256]{1,0:T(8,128)(2,1)S(1)}) custom-call(bf16[512,1024]{1,0:T(8,128)(2,1)} %q_hbm.1, bf16[512,256]{1,0:T(8,128)(2,1)} %kv_hbm.1, s32[2,4]{1,0:T(2,128)} %bitcast.1, s32[512]{0:T(512)} %pos_hbm.1), custom_call_target="tpu_custom_call" | custom-call | tf_op jit(solution)/shard_map/span_attention/pallas_call | solution.py:329
  31.8 1.5 %last_values.1 = bf16[512,1024]{1,0:T(8,128)(2,1)} custom-call(f32[8,512,256]{2,1,0:T(8,128)S(1)} %get-tuple-element.9.acc, f32[8,512,128]{2,1,0:T(8,128)S(1)} %get-tuple-element.10.alpha, bf16[8,512,256]{2,1,0:T(8,128)(2,1)S(1)} %get-tuple-element.11.weights, bf16[256,256]{1,0:T(8,128)(2,1)S(1)} %get-tuple-element.12.va), custom_call_target="tpu_custom_call" | custom-call | tf_op jit(solution)/shard_map/last_values/pallas_call | solution.py:363
